TPU v7x, 32 devices: a whole 2x2x4 slice. The times are simulated.
32 devices in a mesh: freq: 4 (over z), tile: 8 (over y, x, core).
Axes of the slice: x: 2, y: 2, z: 4, core: 2. Of those that a mesh axis runs over, the one named last changes fastest.
Arguments:
- sources: bfloat16 [4, 2, 4096, 256], P('freq', None, 'tile'), may hold values from -6 to 6
- u_factor: bfloat16 [4, 2, 4096, 1024], P('freq', None, 'tile'), may hold values from -0.125 to 0.125
- v_factor: bfloat16 [4, 2, 4096, 1024], P('freq', None, 'tile'), may hold values from -0.25 to 0.25
- tile_ranks: int32 [16, 16], replicated, may hold values from 32 to 64
- window_start: int32 [4096], P('tile'), may hold values from 0 to 3
- window_end: int32 [4096], P('tile'), may hold values from 5 to 8
Outputs:
- adjoint: bfloat16 [4, 2, 4096, 256], P('freq', None, 'tile')
Inputs may be any that keep to these rules, and one draw needn't show every extreme that they name: `tile_ranks`: the number of leading coefficients of tile (i, j) in use.
All inputs are finite; a program needn't handle non-finite values.
Results may differ from a plain program's by a relative error of at most 0.01.
Values may be sent and summed in bfloat16 or wider, within the bound.
A program may use at most 128 MiB of HBM per device.

v0:
```python
import math

import jax
import jax.numpy as jnp
from jax import lax
from jax.sharding import PartitionSpec as P

B = 256
R = 64
FREQ_DEV = 1
T_DEV = 2


def product(pattern, left_op, right_op):
    return jnp.einsum(pattern, left_op, right_op, preferred_element_type=jnp.float32)


def precise(pattern, left_op, right_op):
    return jnp.einsum(pattern, left_op, right_op, precision=lax.Precision.HIGHEST)


def phase_tables(freq_count, time_count):
    moment = jnp.arange(time_count, dtype=jnp.int32)[:, None]
    freq_col = jnp.arange(freq_count, dtype=jnp.int32)[None, :]
    angles = (moment * freq_col % time_count).astype(jnp.float32) * (2.0 * math.pi / time_count)
    scaling = 1.0 / math.sqrt(freq_count)
    return (jnp.cos(angles) * scaling, jnp.sin(angles) * scaling)


def on_device(sources, u_factor, v_factor, tile_ranks, window_start, window_end):
    row_span = sources.shape[2]
    shot_count = sources.shape[3]
    local_tiles = row_span // B
    all_tiles = u_factor.shape[3] // R
    first_tile = lax.axis_index("tile") * local_tiles
    retained = (jnp.arange(R, dtype=jnp.int32)[None, None, :] < tile_ranks[:, :, None]).astype(
        jnp.float32
    )
    retained_rows = lax.dynamic_slice_in_dim(retained, first_tile, local_tiles, 0)
    u_tiles = u_factor[0].reshape(2, local_tiles, B, all_tiles, R)
    v_tiles = v_factor[0].reshape(2, local_tiles, B, all_tiles, R)
    retained_cols = lax.dynamic_slice_in_dim(retained, first_tile, local_tiles, 1)
    shot_data = sources[0].reshape(2, local_tiles, B, shot_count)
    real_part = product("jbir,jbs->ijrs", v_tiles[0], shot_data[0]) + product(
        "jbir,jbs->ijrs", v_tiles[1], shot_data[1]
    )
    imag_part = product("jbir,jbs->ijrs", v_tiles[0], shot_data[1]) - product(
        "jbir,jbs->ijrs", v_tiles[1], shot_data[0]
    )
    coefficients = (jnp.stack([real_part, imag_part]) * retained_cols[None, :, :, :, None]).astype(
        jnp.bfloat16
    )
    coefficients = lax.all_to_all(coefficients, "tile", split_axis=1, concat_axis=2, tiled=True)
    data_real = product("ibjr,ijrs->ibs", u_tiles[0], coefficients[0]) - product(
        "ibjr,ijrs->ibs", u_tiles[1], coefficients[1]
    )
    data_imag = product("ibjr,ijrs->ibs", u_tiles[0], coefficients[1]) + product(
        "ibjr,ijrs->ibs", u_tiles[1], coefficients[0]
    )
    recorded = (
        jnp.stack([data_real, data_imag]).reshape(2, row_span, shot_count).astype(jnp.bfloat16)
    )
    groups = lax.axis_size("freq")
    freq_index = lax.axis_index("freq")
    time_count = T_DEV * groups
    cos_table, sin_table = phase_tables(FREQ_DEV * groups, time_count)
    row_piece = row_span // groups
    regrouped = lax.all_to_all(
        recorded[None], "freq", split_axis=2, concat_axis=0, tiled=True
    ).astype(jnp.float32)
    start_rows = lax.dynamic_slice_in_dim(window_start, freq_index * row_piece, row_piece, 0)
    end_rows = lax.dynamic_slice_in_dim(window_end, freq_index * row_piece, row_piece, 0)
    time_real = precise("tf,fns->tns", cos_table, regrouped[:, 0]) - precise(
        "tf,fns->tns", sin_table, regrouped[:, 1]
    )
    time_imag = precise("tf,fns->tns", cos_table, regrouped[:, 1]) + precise(
        "tf,fns->tns", sin_table, regrouped[:, 0]
    )
    moments = jnp.arange(time_count, dtype=jnp.int32)[:, None]
    window = ((moments >= start_rows[None, :]) & (moments < end_rows[None, :])).astype(jnp.float32)[
        :, :, None
    ]
    time_real = time_real * window
    time_imag = time_imag * window
    back_real = precise("tf,tns->fns", cos_table, time_real) + precise(
        "tf,tns->fns", sin_table, time_imag
    )
    back_imag = precise("tf,tns->fns", cos_table, time_imag) - precise(
        "tf,tns->fns", sin_table, time_real
    )
    windowed = jnp.stack([back_real, back_imag], axis=1).astype(jnp.bfloat16)
    windowed = lax.all_to_all(windowed, "freq", split_axis=0, concat_axis=2, tiled=True)[0]
    w_grid = windowed.reshape(2, local_tiles, B, shot_count)
    adj_real = product("ibjr,ibs->ijrs", u_tiles[0], w_grid[0]) + product(
        "ibjr,ibs->ijrs", u_tiles[1], w_grid[1]
    )
    adj_imag = product("ibjr,ibs->ijrs", u_tiles[0], w_grid[1]) - product(
        "ibjr,ibs->ijrs", u_tiles[1], w_grid[0]
    )
    adj_coef = (jnp.stack([adj_real, adj_imag]) * retained_rows[None, :, :, :, None]).astype(
        jnp.bfloat16
    )
    adj_coef = lax.all_to_all(adj_coef, "tile", split_axis=2, concat_axis=1, tiled=True)
    out_real = product("jbir,ijrs->jbs", v_tiles[0], adj_coef[0]) - product(
        "jbir,ijrs->jbs", v_tiles[1], adj_coef[1]
    )
    out_imag = product("jbir,ijrs->jbs", v_tiles[0], adj_coef[1]) + product(
        "jbir,ijrs->jbs", v_tiles[1], adj_coef[0]
    )
    return jnp.stack([out_real, out_imag]).reshape(1, 2, row_span, shot_count).astype(jnp.bfloat16)


def solution(mesh):
    in_specs = (
        P("freq", None, "tile", None),
        P("freq", None, "tile", None),
        P("freq", None, "tile", None),
        P(),
        P("tile"),
        P("tile"),
    )
    out_specs = P("freq", None, "tile", None)
    return jax.shard_map(
        on_device, mesh=mesh, in_specs=in_specs, out_specs=out_specs, check_vma=False
    )
```

profile of v0, /device:TPU:0, one launch (start us, length us, event | category | flops | bytes accessed | tf_op | source)
XLA Modules:
  0.0 150.7 jit_solution(6045488058576202176)
XLA Ops:
  0.0 2.7 %fusion.77 = (bf16[1,1,512,1024]{3,2,1,0:T(8,128)(2,1)}, bf16[1,1,512,1024]{3,2,1,0:T(8,128)(2,1)S(1)}) fusion(bf16[1,2,512,1024]{3,2,1,0:T(8,128)(2,1)} %param.8), kind=kLoop, calls=%fused_computation.114 | loop fusion | bytes 4194304 | tf_op jit(solution)/shard_map/slice | solution.py:45
  2.7 1.3 reshape.170
  4.0 1.7 %copy.75 = bf16[2,256,16,64]{1,3,2,0:T(8,128)(2,1)S(1)} copy(bf16[2,256,16,64]{3,2,1,0:T(8,128)(2,1)S(1)} %reshape.170) | data formatting | bytes 2097152 | tf_op jit(solution)/shard_map/squeeze | solution.py:104
  5.7 1.1 fusion.79
  6.8 4.0 %reshape.171 = bf16[2,256,16,64]{3,2,1,0:T(8,128)(2,1)} reshape(bf16[1,1,512,1024]{3,2,1,0:T(8,128)(2,1)} %get-tuple-element.11) | data formatting | bytes 2097152 | tf_op jit(solution)/shard_map/squeeze | solution.py:45
  10.8 2.8 %copy.77 = bf16[2,256,16,64]{1,3,2,0:T(8,128)(2,1)S(1)} copy(bf16[2,256,16,64]{3,2,1,0:T(8,128)(2,1)} %reshape.171) | data formatting | bytes 2097152 | tf_op jit(solution)/shard_map/squeeze | solution.py:45
  13.6 1.8 %fusion.82 = f32[2,256,1024]{1,2,0} fusion(bf16[2,256,1024]{1,2,0:T(8,128)(2,1)S(1)} %bitcast.189, bf16[2,256,256]{2,1,0:T(8,128)(2,1)S(1)} %bitcast.216), kind=kOutput, calls=%fused_computation.119 | convolution fusion | flops 268435456 | bytes 3407872
  15.4 1.8 %fusion.80 = f32[2,256,1024]{1,2,0} fusion(bf16[2,256,1024]{1,2,0:T(8,128)(2,1)S(1)} %bitcast.190, bf16[2,256,256]{2,1,0:T(8,128)(2,1)S(1)} %bitcast.218), kind=kOutput, calls=%fused_computation.117 | convolution fusion | flops 268435456 | bytes 3407872
  17.1 1.8 %fusion.83 = f32[2,256,1024]{1,2,0} fusion(bf16[2,256,1024]{1,2,0:T(8,128)(2,1)S(1)} %bitcast.185, bf16[2,256,256]{2,1,0:T(8,128)(2,1)S(1)} %bitcast.219), kind=kOutput, calls=%fused_computation.120 | convolution fusion | flops 268435456 | bytes 3407872
  18.9 1.8 %fusion.81 = f32[2,256,1024]{1,2,0} fusion(bf16[2,256,1024]{1,2,0:T(8,128)(2,1)S(1)} %bitcast.186, bf16[2,256,256]{2,1,0:T(8,128)(2,1)S(1)} %bitcast.217), kind=kOutput, calls=%fused_computation.118 | convolution fusion | flops 268435456 | bytes 3407872
  20.9 4.3 %subtract_bitcast_fusion.1 = (f32[1,16,2,64,256]{4,3,1,2,0:T(8,128)S(1)}, f32[1,16,2,64,256]{4,3,1,2,0:T(8,128)S(1)}) fusion(f32[2,256,16,64]{1,3,2,0:T(8,128)} %bitcast.208, f32[2,256,16,64]{1,3,2,0:T(8,128)} %bitcast.210, f32[2,256,16,64]{1,3,2,0:T(8,128)} %bitcast.209, f32[2,256,16,64]{1,3,2,0:T(8,128)} %bitcast.211), kind=kLoop, calls=%fused_computation.8 | loop fusion | flops 1048576 | bytes 12582912 | tf_op jit(solution)/shard_map/stack | solution.py:50
  25.6 1.6 %copy.81 = bf16[2,16,2,64,256]{4,3,2,0,1:T(8,128)(2,1)} copy(bf16[2,16,2,64,256]{4,3,1,2,0:T(8,128)(2,1)S(1)} %fusion) | data formatting | bytes 4194304 | tf_op jit(solution)/shard_map/convert_element_type | solution.py:50
  27.2 5.2 %all-to-all-start = ((bf16[2,16,2,64,256]{4,3,2,0,1:T(8,128)(2,1)}), bf16[2,16,2,64,256]{4,3,2,0,1:T(8,128)(2,1)}, u32[]{:S(2)}, u32[]{:S(2)}) async-start(bf16[2,16,2,64,256]{4,3,2,0,1:T(8,128)(2,1)} %copy.81), calls=%async_computation | async-start | bytes 4194304 | tf_op jit(solution)/shard_map/all_to_all | solution.py:53
  32.3 2.7 %fusion.76 = (bf16[1,1,512,1024]{3,2,1,0:T(8,128)(2,1)S(1)}, bf16[1,1,512,1024]{3,2,1,0:T(8,128)(2,1)}) fusion(bf16[1,2,512,1024]{3,2,1,0:T(8,128)(2,1)} %param.7), kind=kLoop, calls=%fused_computation.113 | loop fusion | bytes 4194304 | tf_op jit(solution)/shard_map/slice | solution.py:55
  35.1 2.3 %reshape.173 = bf16[2,256,16,64]{3,2,1,0:T(8,128)(2,1)} reshape(bf16[1,1,512,1024]{3,2,1,0:T(8,128)(2,1)S(1)} %get-tuple-element.9) | data formatting | bytes 2097152 | tf_op jit(solution)/shard_map/squeeze | solution.py:55
  37.4 2.8 %copy.86 = bf16[2,256,16,64]{1,3,2,0:T(8,128)(2,1)S(1)} copy(bf16[2,256,16,64]{3,2,1,0:T(8,128)(2,1)} %reshape.173) | data formatting | bytes 2097152 | tf_op jit(solution)/shard_map/squeeze | solution.py:55
  40.2 4.0 %reshape.172 = bf16[2,256,16,64]{3,2,1,0:T(8,128)(2,1)} reshape(bf16[1,1,512,1024]{3,2,1,0:T(8,128)(2,1)} %get-tuple-element.10) | data formatting | bytes 2097152 | tf_op jit(solution)/shard_map/squeeze | solution.py:94
  44.2 3.5 %copy.84 = bf16[2,256,16,64]{1,3,2,0:T(8,128)(2,1)} copy(bf16[2,256,16,64]{3,2,1,0:T(8,128)(2,1)} %reshape.172) | data formatting | bytes 2097152 | tf_op jit(solution)/shard_map/squeeze | solution.py:94
  47.7 11.3 %all-to-all-done = bf16[2,16,2,64,256]{4,3,2,0,1:T(8,128)(2,1)} async-done(((bf16[2,16,2,64,256]{4,3,2,0,1:T(8,128)(2,1)}), bf16[2,16,2,64,256]{4,3,2,0,1:T(8,128)(2,1)}, u32[]{:S(2)}, u32[]{:S(2)}) %all-to-all-start) | async-done | bytes 2097184 | tf_op jit(solution)/shard_map/all_to_all | solution.py:53
  59.1 1.7 %copy.130 = bf16[2,8,2,2,64,256]{5,4,3,1,2,0:T(8,128)(2,1)S(1)} copy(bf16[2,8,2,2,64,256]{5,4,3,0,2,1:T(8,128)(2,1)} %bitcast.15) | data formatting | bytes 4194304 | tf_op jit(solution)/shard_map/all_to_all | solution.py:53
  64.2 2.0 %pad_maximum_fusion = bf16[1,2,512,256]{3,1,0,2:T(2,128)(2,1)} fusion(bf16[1,1,512,256]{3,1,0,2:T(2,128)(2,1)S(1)} %copy.90, bf16[1,1,512,256]{3,1,0,2:T(2,128)(2,1)S(1)} %copy.89), kind=kLoop, calls=%fused_computation.36 | loop fusion | flops 1048576 | bytes 1048576 | tf_op jit(solution)/shard_map/stack | solution.py:61
  66.2 5.4 %all-to-all-start.1 = ((bf16[1,2,512,256]{3,1,0,2:T(2,128)(2,1)}), bf16[1,2,512,256]{3,1,0,2:T(2,128)(2,1)}, u32[]{:S(2)}, u32[]{:S(2)}) async-start(bf16[1,2,512,256]{3,1,0,2:T(2,128)(2,1)} %pad_maximum_fusion), calls=%async_computation.1 | async-start | bytes 1048576 | tf_op jit(solution)/shard_map/all_to_all | solution.py:68
  73.2 9.9 %all-to-all-done.1 = bf16[1,2,512,256]{3,1,0,2:T(2,128)(2,1)} async-done(((bf16[1,2,512,256]{3,1,0,2:T(2,128)(2,1)}), bf16[1,2,512,256]{3,1,0,2:T(2,128)(2,1)}, u32[]{:S(2)}, u32[]{:S(2)}) %all-to-all-start.1) | async-done | bytes 524320 | tf_op jit(solution)/shard_map/all_to_all | solution.py:68
  83.1 1.4 copy.131
  86.9 1.0 fusion.31
  88.8 1.0 fusion.28
  89.8 1.1 fusion.15
  90.9 1.1 fusion.14
  93.2 4.1 %all-to-all-start.2 = ((bf16[4,2,128,256]{3,2,1,0:T(8,128)(2,1)}), bf16[4,2,128,256]{3,2,1,0:T(8,128)(2,1)}, u32[]{:S(2)}, u32[]{:S(2)}) async-start(bf16[4,2,128,256]{3,2,1,0:T(8,128)(2,1)} %copy.94), calls=%async_computation.2 | async-start | bytes 1048576 | tf_op jit(solution)/shard_map/all_to_all | solution.py:92
  97.4 11.4 %all-to-all-done.2 = bf16[4,2,128,256]{3,2,1,0:T(8,128)(2,1)} async-done(((bf16[4,2,128,256]{3,2,1,0:T(8,128)(2,1)}), bf16[4,2,128,256]{3,2,1,0:T(8,128)(2,1)}, u32[]{:S(2)}, u32[]{:S(2)}) %all-to-all-start.2) | async-done | bytes 524320 | tf_op jit(solution)/shard_map/all_to_all | solution.py:92
  108.8 1.2 copy.132
  113.1 34.1 %all_to_all.63 = bf16[2,2,16,64,256]{4,3,1,0,2:T(8,128)(2,1)S(1)} all-to-all(bf16[2,2,16,64,256]{4,3,1,0,2:T(8,128)(2,1)S(1)} %copy.101), channel_id=1, replica_groups=mesh['freq'=4,'tile'=8] {'tile'}, dimensions={2} | all-to-all | bytes 4194304 | tf_op jit(solution)/shard_map/all_to_all | solution.py:103
  (45 shorter events, 16.5 us)
Async XLA Ops:
  18.9 1.8 %copy-start.2 = (s32[16,16]{1,0:T(8,128)S(1)}, s32[16,16]{1,0:T(8,128)}, u32[]{:S(2)}) copy-start(s32[16,16]{1,0:T(8,128)} %param.9) | copy-start | bytes 3076
  27.2 31.9 %all-to-all-start = ((bf16[2,16,2,64,256]{4,3,2,0,1:T(8,128)(2,1)}), bf16[2,16,2,64,256]{4,3,2,0,1:T(8,128)(2,1)}, u32[]{:S(2)}, u32[]{:S(2)}) async-start(bf16[2,16,2,64,256]{4,3,2,0,1:T(8,128)(2,1)} %copy.81), calls=%async_computation | async-start | bytes 4194304 | tf_op jit(solution)/shard_map/all_to_all | solution.py:53
  61.1 1.2 copy-start
  66.2 16.9 %all-to-all-start.1 = ((bf16[1,2,512,256]{3,1,0,2:T(2,128)(2,1)}), bf16[1,2,512,256]{3,1,0,2:T(2,128)(2,1)}, u32[]{:S(2)}, u32[]{:S(2)}) async-start(bf16[1,2,512,256]{3,1,0,2:T(2,128)(2,1)} %pad_maximum_fusion), calls=%async_computation.1 | async-start | bytes 1048576 | tf_op jit(solution)/shard_map/all_to_all | solution.py:68
  93.2 15.6 %all-to-all-start.2 = ((bf16[4,2,128,256]{3,2,1,0:T(8,128)(2,1)}), bf16[4,2,128,256]{3,2,1,0:T(8,128)(2,1)}, u32[]{:S(2)}, u32[]{:S(2)}) async-start(bf16[4,2,128,256]{3,2,1,0:T(8,128)(2,1)} %copy.94), calls=%async_computation.2 | async-start | bytes 1048576 | tf_op jit(solution)/shard_map/all_to_all | solution.py:92
  108.8 1.4 copy-start.1
where the time goes:
time: 151 us
  local copies, waits for them, and re-layouts  39.4 us (26%)
  blocking collectives  34.1 us (23%)
  waiting for transfers between devices  32.6 us (22%)
  matrix products  20.4 us (14%)
  starting transfers between devices  14.7 us (10%)
  other arithmetic  9.09 us (6%)
    all_to_all x1, blocking collectives, on_device(): lax.all_to_all(adj_coef, 'tile', split_axis=2, concat_axis=1, tiled=True)  34.1 us
    all_to_all x1, waiting for transfers between devices, on_device(): lax.all_to_all(windowed, 'freq', split_axis=0, concat_axis=2, tiled=True)[0]  11.4 us
    all_to_all x1, waiting for transfers between devices, on_device(): lax.all_to_all(coefficients, 'tile', split_axis=1, concat_axis=2, tiled=T...  11.3 us
    all_to_all x1, waiting for transfers between devices, on_device(): lax.all_to_all(recorded[None], 'freq', split_axis=2, concat_axis=0, tiled...  9.91 us
    unnamed x8, matrix products  8.8 us
    squeeze x2, local copies, waits for them, and re-layouts, on_device(): u_tiles[0]  7.57 us
    dot_general x8, matrix products, precise(): jnp.einsum(pattern, left_op, right_op, precision=lax.Precision.HIGHEST)  7.32 us
    squeeze x2, local copies, waits for them, and re-layouts, on_device(): v_tiles[1]  6.81 us
  transfers between devices with their start and end apart: 3, of which 3 were waited for; matrix products, arithmetic and copies ran while one was open for 11% of the time, Pallas kernels for 0%

commit v1 on v0

v1 whole, which is shorter than its diff:
```python
import functools
import math

import jax
import jax.numpy as jnp
from jax import lax
from jax.experimental import pallas as pl
from jax.experimental.pallas import tpu as pltpu
from jax.sharding import PartitionSpec as P

B = 256
R = 64
CHUNKS = 2
MESH = pl.DeviceIdType.MESH


def dot(a, b):
    return jnp.dot(a, b, preferred_element_type=jnp.float32)


def dot_nt(a, b):
    return lax.dot_general(a, b, (((1,), (1,)), ((), ())), preferred_element_type=jnp.float32)


def kernel(
    n, groups, src_hbm, u_hbm, v_hbm, ranks, start_ref, end_ref, out_ref,
    src, u, v, xt, t_out, t_in, z_out, z_in, kbuf,
    in_sem, t_send, t_recv, z_send, z_recv,
):
    me = lax.axis_index("tile")
    mf = lax.axis_index("freq")
    span = src.shape[1]
    shots = src.shape[2]
    tiles = span // B
    lanes = tiles * R
    chunks = t_out.shape[1]
    width = shots // chunks
    piece = width // groups
    pairs = n // 2
    my_pair = lax.div(me, 2)
    sibling = me + 1 - 2 * lax.rem(me, 2)

    barrier = pltpu.get_barrier_semaphore()
    for r in range(1, n):
        pl.semaphore_signal(barrier, inc=1, device_id=(mf, lax.rem(me + r, n)), device_id_type=MESH)
    for r in range(1, groups):
        pl.semaphore_signal(
            barrier, inc=1, device_id=(lax.rem(mf + r, groups), me), device_id_type=MESH
        )
    loads = [
        pltpu.make_async_copy(a, b, in_sem.at[k])
        for k, (a, b) in enumerate(((src_hbm, src), (v_hbm, v), (u_hbm, u)))
    ]
    for copy in loads:
        copy.start()

    times = 2 * groups
    first, last = start_ref[...], end_ref[...]
    inside = [((first <= t) & (last > t)).astype(jnp.float32) for t in range(times)]
    for d in range(groups):
        real = imag = jnp.zeros_like(inside[0])
        for t in range(times):
            angle = 2.0 * math.pi * ((t * d) % times) / times
            real += inside[t] * (math.cos(angle) / groups)
            imag += inside[t] * (math.sin(angle) / groups)
        kbuf[2 * d] = real
        kbuf[2 * d + 1] = imag

    loads[0].wait()
    for c in range(chunks):
        for j in range(tiles):
            part = [
                src[k, j * B : (j + 1) * B, c * width : (c + 1) * width].astype(jnp.float32).T
                for k in range(2)
            ]
            xt[c, j, 0, :width] = part[0].astype(jnp.bfloat16)
            xt[c, j, 0, width:] = part[1].astype(jnp.bfloat16)
            xt[c, j, 1, :width] = part[1].astype(jnp.bfloat16)
            xt[c, j, 1, width:] = (-part[0]).astype(jnp.bfloat16)
    loads[1].wait()

    lane = lax.broadcasted_iota(jnp.int32, (1, lanes), 1)
    low = lane < R
    within = lax.rem(lane, R)

    def t_copy(phase, c, r):
        pair = lax.rem(my_pair + lax.div(r, 2), pairs)
        target = jnp.where(lax.div(r, 2) == 0, sibling, 2 * pair + lax.rem(r, 2))
        return pltpu.make_async_remote_copy(
            src_ref=t_out.at[phase, c, target],
            dst_ref=t_in.at[phase, c, me],
            send_sem=t_send.at[phase, c, r],
            recv_sem=t_recv.at[phase, c, me],
            device_id=(mf, target),
            device_id_type=MESH,
        )

    def t_arrived(phase, c, source):
        return pltpu.make_async_remote_copy(
            src_ref=t_out.at[phase, c, source],
            dst_ref=t_in.at[phase, c, source],
            send_sem=t_send.at[phase, c, 0],
            recv_sem=t_recv.at[phase, c, source],
            device_id=(mf, source),
            device_id_type=MESH,
        )

    def blocks(phase, c, pair, operands, weights, put):
        columns = pl.ds(pl.multiple_of(pair * 2 * lanes, 2 * lanes), 2 * lanes)
        full = [
            dot(operands(k, 0), weights[0, k * B : (k + 1) * B, columns])
            + dot(operands(k, 1), weights[1, k * B : (k + 1) * B, columns])
            for k in range(tiles)
        ]
        for h in range(2):
            dest = 2 * pair + h
            own, other = (f[:, h * lanes : (h + 1) * lanes] for f in full)
            mixed = (
                jnp.where(low, own, pltpu.roll(other, R, 1)),
                jnp.where(low, pltpu.roll(own, R, 1), other),
            )
            for k in range(tiles):
                theirs = dest * tiles + k
                if phase == 0:
                    rank = [ranks[theirs, me * tiles + m] for m in range(tiles)]
                else:
                    rank = [ranks[me * tiles + m, theirs] for m in range(tiles)]
                keep = within < jnp.where(low, rank[0], rank[1])
                put(dest, k, jnp.where(keep, mixed[k], 0.0).astype(jnp.bfloat16))

    def produce(phase, c, operands, weights, begin, before=None):
        def put(dest, k, value):
            t_out[phase, c, dest, k] = value

        def step(k, carry):
            blocks(phase, c, lax.rem(my_pair + k, pairs), operands, weights, put)
            for h in range(2):
                if before is not None:
                    before(2 * k + h)
                if begin:
                    t_copy(phase, c, 2 * k + h).start()
            return carry

        lax.fori_loop(1, pairs, step, 0)
        blocks(phase, c, my_pair, operands, weights, put)
        t_in[phase, c, me] = t_out[phase, c, me]
        if before is not None:
            before(0)
        if begin:
            t_copy(phase, c, 0).start()

    def each_send(do):
        def step(r, carry):
            do(r)
            return carry

        lax.fori_loop(2, n, step, 0)
        do(0)

    def await_tiles(phase, c):
        def step(r, carry):
            t_arrived(phase, c, lax.rem(me + r, n)).wait_recv()
            return carry

        lax.fori_loop(1, n, step, 0)

    def gathered(phase, c, k):
        whole = jnp.concatenate([t_in[phase, c, s, k] for s in range(n)], axis=1)
        turned = jnp.concatenate([-whole[width:], whole[:width]], axis=0)
        return whole, turned

    def z_copy(phase, c, r):
        target = lax.rem(mf + r, groups)
        return pltpu.make_async_remote_copy(
            src_ref=z_out.at[phase, c, target],
            dst_ref=z_in.at[phase, c, mf],
            send_sem=z_send.at[phase, c, r],
            recv_sem=z_recv.at[phase, c, mf],
            device_id=(target, me),
            device_id_type=MESH,
        )

    def z_arrived(phase, c, source):
        return pltpu.make_async_remote_copy(
            src_ref=z_out.at[phase, c, source],
            dst_ref=z_in.at[phase, c, source],
            send_sem=z_send.at[phase, c, 0],
            recv_sem=z_recv.at[phase, c, source],
            device_id=(source, me),
            device_id_type=MESH,
        )

    def z_start(phase, c):
        for r in range(1, groups):
            z_copy(phase, c, r).start()
        z_in[phase, c, mf] = z_out[phase, c, mf]

    def z_wait(phase, c):
        for r in range(1, groups):
            z_arrived(phase, c, lax.rem(mf + r, groups)).wait_recv()

    def record(c):
        for i in range(tiles):
            whole, turned = gathered(0, c, i)
            rows = slice(i * B, (i + 1) * B)
            result = (dot_nt(whole, u[0, rows, :]) + dot_nt(turned, u[1, rows, :])).astype(
                jnp.bfloat16
            )
            for g in range(groups):
                for k in range(2):
                    at = k * width + g * piece
                    z_out[0, c, g, k, :, rows] = result[at : at + piece]

    def window(c):
        def step(b, carry):
            at = pl.ds(pl.multiple_of(b * 128, 128), 128)
            factor = [kbuf[d, :, at] for d in range(2 * groups)]
            for row in range(0, piece, 16):
                rows = slice(row, row + 16)
                data = [
                    [z_in[0, c, f, k, rows, at].astype(jnp.float32) for k in range(2)]
                    for f in range(groups)
                ]
                for f in range(groups):
                    real, imag = data[f][0] * factor[0], data[f][1] * factor[0]
                    for g in range(groups):
                        if g == f:
                            continue
                        kr, ki = factor[2 * abs(g - f)], factor[2 * abs(g - f) + 1]
                        if g > f:
                            real += kr * data[g][0] - ki * data[g][1]
                            imag += kr * data[g][1] + ki * data[g][0]
                        else:
                            real += kr * data[g][0] + ki * data[g][1]
                            imag += kr * data[g][1] - ki * data[g][0]
                    z_out[1, c, f, 0, rows, at] = real.astype(jnp.bfloat16)
                    z_out[1, c, f, 1, rows, at] = imag.astype(jnp.bfloat16)
            return carry

        lax.fori_loop(0, span // 128, step, 0)

    def shot_operand(c):
        return lambda k, which: xt[c, k, which]

    def data_operand(c):
        for i in range(tiles):
            cols = slice(i * B, (i + 1) * B)
            part = [z_in[1, c, :, k, :, cols].reshape(width, B) for k in range(2)]
            xt[c, i, 0, :width] = part[0]
            xt[c, i, 0, width:] = part[1]
            xt[c, i, 1, :width] = part[1]
            xt[c, i, 1, width:] = -part[0]
        return shot_operand(c)

    def finish(c):
        columns = slice(c * width, (c + 1) * width)
        for j in range(tiles):
            whole, turned = gathered(1, c, j)
            rows = slice(j * B, (j + 1) * B)
            result = (dot_nt(v[0, rows, :], whole) + dot_nt(v[1, rows, :], turned)).astype(
                jnp.bfloat16
            )
            out_ref[0, rows, columns] = result[:, :width]
            out_ref[1, rows, columns] = result[:, width:]

    pl.semaphore_wait(barrier, n + groups - 2)
    produce(0, 0, shot_operand(0), v, True)
    for c in range(1, chunks):
        produce(0, c, shot_operand(c), v, False)

    def follow(phase, c):
        def do(r):
            t_copy(phase, c - 1, r).wait_send()
            t_copy(phase, c, r).start()

        each_send(do)

    loads[2].wait()
    for c in range(chunks):
        if c + 1 < chunks:
            follow(0, c + 1)
        await_tiles(0, c)
        record(c)
        z_start(0, c)
        if c > 0:
            z_wait(1, c - 1)
            produce(1, c - 1, data_operand(c - 1), u, True)
        z_wait(0, c)
        window(c)
        z_start(1, c)
    z_wait(1, chunks - 1)
    produce(1, chunks - 1, data_operand(chunks - 1), u, True)
    for c in range(chunks):
        await_tiles(1, c)
        finish(c)

    each_send(lambda r: t_copy(0, chunks - 1, r).wait_send())
    for c in range(chunks):
        each_send(functools.partial(lambda c, r: t_copy(1, c, r).wait_send(), c))
        for phase in range(2):
            for r in range(1, groups):
                z_copy(phase, c, r).wait_send()


def on_device(sources, u_factor, v_factor, tile_ranks, window_start, window_end):
    n = lax.axis_size("tile")
    groups = lax.axis_size("freq")
    span, shots = sources.shape[2:]
    depth = u_factor.shape[3]
    tiles = span // B
    width = shots // CHUNKS
    piece = width // groups
    lanes = tiles * R
    flops = 4 * 8 * span * depth * shots
    bf16 = jnp.bfloat16
    dma = pltpu.SemaphoreType.DMA
    anywhere = pl.BlockSpec(memory_space=pl.ANY)
    vmem = pl.BlockSpec(memory_space=pltpu.VMEM)
    out = pl.pallas_call(
        functools.partial(kernel, n, groups),
        out_shape=jax.ShapeDtypeStruct((2, span, shots), bf16),
        in_specs=[
            anywhere, anywhere, anywhere, pl.BlockSpec(memory_space=pltpu.SMEM), vmem, vmem,
        ],
        out_specs=vmem,
        scratch_shapes=[
            pltpu.VMEM((2, span, shots), bf16),
            pltpu.VMEM((2, span, depth), bf16),
            pltpu.VMEM((2, span, depth), bf16),
            pltpu.VMEM((CHUNKS, tiles, 2, 2 * width, B), bf16),
            pltpu.VMEM((2, CHUNKS, n, tiles, 2 * width, lanes), bf16),
            pltpu.VMEM((2, CHUNKS, n, tiles, 2 * width, lanes), bf16),
            pltpu.VMEM((2, CHUNKS, groups, 2, piece, span), bf16),
            pltpu.VMEM((2, CHUNKS, groups, 2, piece, span), bf16),
            pltpu.VMEM((2 * groups, 1, span), jnp.float32),
            dma((3,)),
            dma((2, CHUNKS, n)),
            dma((2, CHUNKS, n)),
            dma((2, CHUNKS, groups)),
            dma((2, CHUNKS, groups)),
        ],
        compiler_params=pltpu.CompilerParams(
            collective_id=0, has_side_effects=True, vmem_limit_bytes=56 * 2**20
        ),
        cost_estimate=pl.CostEstimate(
            flops=flops, bytes_accessed=4 * span * (2 * depth + 2 * shots), transcendentals=0
        ),
    )(
        sources[0], u_factor[0], v_factor[0], tile_ranks,
        window_start.reshape(1, span), window_end.reshape(1, span),
    )
    return out[None]


def solution(mesh):
    wide = P("freq", None, "tile", None)
    return jax.shard_map(
        on_device, mesh=mesh, in_specs=(wide, wide, wide, P(), P("tile"), P("tile")),
        out_specs=wide, check_vma=False,
    )
```

time: 151 us -> 65.7 us (0.44)
  the two profiles are of different devices: /device:TPU:0 before, /device:TPU:25 now
where the time goes in v1:
time: 65.7 us; the launch traced here: 65.5 us
  Pallas kernels  63.7 us (97%)
  local copies, waits for them, and re-layouts  1.87 us (3%)
    pallas_call x1, Pallas kernels, on_device(): pl.pallas_call(functools.partial(kernel, n, groups), out_shape=jax.ShapeD...  63.7 us
    unnamed x1, local copies, waits for them, and re-layouts  1.87 us

profile of v1, /device:TPU:25, one launch (start us, length us, event | category | flops | bytes accessed | tf_op | source)
XLA Modules:
  0.0 65.5 jit_solution(14140436794886030975)
XLA Ops:
  0.0 63.7 %shard_map.64 = bf16[2,512,256]{2,1,0:T(8,128)(2,1)} custom-call(bf16[2,512,256]{2,1,0:T(8,128)(2,1)} %bitcast.9, bf16[2,512,1024]{2,1,0:T(8,128)(2,1)} %bitcast.7, bf16[2,512,1024]{2,1,0:T(8,128)(2,1)} %bitcast.8, s32[16,16]{1,0:T(8,128)} %ranks.1, s32[1,512]{1,0:T(1,128)} %bitcast.10, s32[1,512]{1,0:T(1,128)} %bitcast.11), custom_call_target="tpu_custom_call" | custom-call | flops 4294967296 | bytes 5242880 | tf_op jit(solution)/shard_map/pallas_call | solution.py:319
  63.7 1.9 %copy.8 = bf16[1,2,512,256]{3,2,1,0:T(8,128)(2,1)} copy(bf16[1,2,512,256]{3,2,1,0:T(8,128)(2,1)} %bitcast.6) | data formatting | bytes 1048576

commit v2 on v1

--- a/solution.py
+++ b/solution.py
@@ -10,7 +10,7 @@
 
 B = 256
 R = 64
-CHUNKS = 2
+LEAD = 4
 MESH = pl.DeviceIdType.MESH
 
 
@@ -128,25 +128,21 @@
                 keep = within < jnp.where(low, rank[0], rank[1])
                 put(dest, k, jnp.where(keep, mixed[k], 0.0).astype(jnp.bfloat16))
 
-    def produce(phase, c, operands, weights, begin, before=None):
+    def produce(phase, c, operands, weights, send):
         def put(dest, k, value):
             t_out[phase, c, dest, k] = value
 
         def step(k, carry):
             blocks(phase, c, lax.rem(my_pair + k, pairs), operands, weights, put)
             for h in range(2):
-                if before is not None:
-                    before(2 * k + h)
-                if begin:
+                if send:
                     t_copy(phase, c, 2 * k + h).start()
             return carry
 
         lax.fori_loop(1, pairs, step, 0)
         blocks(phase, c, my_pair, operands, weights, put)
         t_in[phase, c, me] = t_out[phase, c, me]
-        if before is not None:
-            before(0)
-        if begin:
+        if send:
             t_copy(phase, c, 0).start()
 
     def each_send(do):
@@ -263,41 +259,36 @@
             out_ref[0, rows, columns] = result[:, :width]
             out_ref[1, rows, columns] = result[:, width:]
 
+    def begin(c):
+        each_send(lambda r: t_copy(0, c, r).start())
+
+    produce(0, 0, shot_operand(0), v, False)
     pl.semaphore_wait(barrier, n + groups - 2)
-    produce(0, 0, shot_operand(0), v, True)
+    begin(0)
     for c in range(1, chunks):
-        produce(0, c, shot_operand(c), v, False)
-
-    def follow(phase, c):
-        def do(r):
-            t_copy(phase, c - 1, r).wait_send()
-            t_copy(phase, c, r).start()
-
-        each_send(do)
-
+        produce(0, c, shot_operand(c), v, c < LEAD)
     loads[2].wait()
+    for step in range(chunks + 4):
+        if step < chunks:
+            await_tiles(0, step)
+            if step + LEAD < chunks:
+                begin(step + LEAD)
+            record(step)
+            z_start(0, step)
+        if 0 <= step - 1 < chunks:
+            z_wait(0, step - 1)
+            window(step - 1)
+            z_start(1, step - 1)
+        if 0 <= step - 2 < chunks:
+            z_wait(1, step - 2)
+            produce(1, step - 2, data_operand(step - 2), u, True)
+        if 0 <= step - 4 < chunks:
+            await_tiles(1, step - 4)
+            finish(step - 4)
+
     for c in range(chunks):
-        if c + 1 < chunks:
-            follow(0, c + 1)
-        await_tiles(0, c)
-        record(c)
-        z_start(0, c)
-        if c > 0:
-            z_wait(1, c - 1)
-            produce(1, c - 1, data_operand(c - 1), u, True)
-        z_wait(0, c)
-        window(c)
-        z_start(1, c)
-    z_wait(1, chunks - 1)
-    produce(1, chunks - 1, data_operand(chunks - 1), u, True)
-    for c in range(chunks):
-        await_tiles(1, c)
-        finish(c)
-
-    each_send(lambda r: t_copy(0, chunks - 1, r).wait_send())
-    for c in range(chunks):
-        each_send(functools.partial(lambda c, r: t_copy(1, c, r).wait_send(), c))
         for phase in range(2):
+            each_send(lambda r, phase=phase, c=c: t_copy(phase, c, r).wait_send())
             for r in range(1, groups):
                 z_copy(phase, c, r).wait_send()
 
@@ -308,7 +299,8 @@
     span, shots = sources.shape[2:]
     depth = u_factor.shape[3]
     tiles = span // B
-    width = shots // CHUNKS
+    chunks = max(1, shots // (16 * groups))
+    width = shots // chunks
     piece = width // groups
     lanes = tiles * R
     flops = 4 * 8 * span * depth * shots
@@ -327,17 +319,17 @@
             pltpu.VMEM((2, span, shots), bf16),
             pltpu.VMEM((2, span, depth), bf16),
             pltpu.VMEM((2, span, depth), bf16),
-            pltpu.VMEM((CHUNKS, tiles, 2, 2 * width, B), bf16),
-            pltpu.VMEM((2, CHUNKS, n, tiles, 2 * width, lanes), bf16),
-            pltpu.VMEM((2, CHUNKS, n, tiles, 2 * width, lanes), bf16),
-            pltpu.VMEM((2, CHUNKS, groups, 2, piece, span), bf16),
-            pltpu.VMEM((2, CHUNKS, groups, 2, piece, span), bf16),
+            pltpu.VMEM((chunks, tiles, 2, 2 * width, B), bf16),
+            pltpu.VMEM((2, chunks, n, tiles, 2 * width, lanes), bf16),
+            pltpu.VMEM((2, chunks, n, tiles, 2 * width, lanes), bf16),
+            pltpu.VMEM((2, chunks, groups, 2, piece, span), bf16),
+            pltpu.VMEM((2, chunks, groups, 2, piece, span), bf16),
             pltpu.VMEM((2 * groups, 1, span), jnp.float32),
             dma((3,)),
-            dma((2, CHUNKS, n)),
-            dma((2, CHUNKS, n)),
-            dma((2, CHUNKS, groups)),
-            dma((2, CHUNKS, groups)),
+            dma((2, chunks, n)),
+            dma((2, chunks, n)),
+            dma((2, chunks, groups)),
+            dma((2, chunks, groups)),
         ],
         compiler_params=pltpu.CompilerParams(
             collective_id=0, has_side_effects=True, vmem_limit_bytes=56 * 2**20

time: 65.7 us -> 58 us (0.88)
  the two profiles are of different devices: /device:TPU:25 before, /device:TPU:0 now
where the time goes in v2:
time: 58 us; the launch traced here: 57.8 us
  Pallas kernels  55.9 us (96%)
  local copies, waits for them, and re-layouts  1.87 us (3%)
    pallas_call x1, Pallas kernels, on_device(): pl.pallas_call(functools.partial(kernel, n, groups), out_shape=jax.ShapeD...  55.9 us
    unnamed x1, local copies, waits for them, and re-layouts  1.87 us

profile of v2, /device:TPU:0, one launch (start us, length us, event | category | flops | bytes accessed | tf_op | source)
XLA Modules:
  0.0 57.8 jit_solution(14918123780106717802)
XLA Ops:
  0.0 55.9 %shard_map.64 = bf16[2,512,256]{2,1,0:T(8,128)(2,1)} custom-call(bf16[2,512,256]{2,1,0:T(8,128)(2,1)} %bitcast.9, bf16[2,512,1024]{2,1,0:T(8,128)(2,1)} %bitcast.7, bf16[2,512,1024]{2,1,0:T(8,128)(2,1)} %bitcast.8, s32[16,16]{1,0:T(8,128)} %ranks.1, s32[1,512]{1,0:T(1,128)} %bitcast.10, s32[1,512]{1,0:T(1,128)} %bitcast.11), custom_call_target="tpu_custom_call" | custom-call | flops 4294967296 | bytes 5242880 | tf_op jit(solution)/shard_map/pallas_call | solution.py:311
  55.9 1.9 %copy.8 = bf16[1,2,512,256]{3,2,1,0:T(8,128)(2,1)} copy(bf16[1,2,512,256]{3,2,1,0:T(8,128)(2,1)} %bitcast.6) | data formatting | bytes 1048576
